TPU v7x, 256 devices: a whole 4x4x8 slice. The times are simulated.
256 devices in a mesh: run: 4 (over y), space: 64 (over z, x, core).
Axes of the slice: x: 4, y: 4, z: 8, core: 2. Of those that a mesh axis runs over, the one named last changes fastest.
Arguments:
- snapshots: bfloat16 [131072, 1024], P('space', 'run'), may hold values from -6 to 6
- run_counts: int32 [4], P('run'), may hold values from 128 to 256
- route_counts: int32 [64, 64], replicated, may hold values from 16 to 48, as said below
Outputs:
- modes: bfloat16 [131072, 256], P('space', 'run')
Inputs may be any that keep to these rules, and one draw needn't show every extreme that they name: route_counts[s, d] depends only on (d - s) mod 64; each of its rows and columns sums to 2048.
All inputs are finite; a program needn't handle non-finite values.
Results may differ from a plain program's by a relative error of at most 0.0069.
The roundings to bfloat16 on the way count: a program that leaves them out, or rounds other values in their place, can miss the bound.
Values may be sent and summed in bfloat16 or wider, within the bound.
No kernel may reach another device: no remote copies, remote signals or barrier semaphores. Data moves between devices by JAX's collectives and lax.ppermute only.
A program may use at most 64 MiB of HBM per device.

v0:
```python
import math

import jax
import jax.numpy as jnp
from jax import lax
from jax.sharding import PartitionSpec as P

ITERS = 2
NS_STEPS = 8


def swapped(block, axis, distance):
    count = lax.axis_size(axis)
    route = []
    for low in range(count):
        high = low | 1 << distance
        if high != low and high < count:
            route += [(low, high), (high, low)]
    return lax.ppermute(block, axis, route)


def route_rows(rows_in, counts_all):
    shards = lax.axis_size("space")
    cell_count = rows_in.shape[0]
    slot_count = 3 * cell_count // (2 * shards)
    own_index = lax.axis_index("space")
    send_counts = lax.dynamic_index_in_dim(counts_all, own_index, 0, keepdims=False)
    send_start = jnp.cumsum(send_counts) - send_counts
    slot_iota = jnp.arange(slot_count, dtype=jnp.int32)
    pick_rows = send_start[:, None] + slot_iota[None, :]
    slot_live = slot_iota[None, :] < send_counts[:, None]
    picked = jnp.take(rows_in, jnp.clip(pick_rows, 0, cell_count - 1).reshape(-1), axis=0)
    picked = picked.reshape(shards, slot_count, rows_in.shape[1])
    outgoing = jnp.where(slot_live[:, :, None], picked, jnp.zeros((), rows_in.dtype))
    incoming = lax.all_to_all(outgoing, "space", split_axis=0, concat_axis=0, tiled=True)
    recv_counts = lax.dynamic_index_in_dim(counts_all, own_index, 1, keepdims=False)
    recv_start = jnp.cumsum(recv_counts) - recv_counts
    places = jnp.arange(cell_count, dtype=jnp.int32)
    before = recv_start[None, :] <= places[:, None]
    source = jnp.sum(before.astype(jnp.int32), axis=1) - 1
    seg_begin = jnp.max(jnp.where(before, recv_start[None, :], 0), axis=1)
    flat_index = source * slot_count + places - seg_begin
    return incoming.reshape(shards * slot_count, rows_in.shape[1])[flat_index]


def start_basis(width):
    eye_block = jnp.eye(width, dtype=jnp.float32)
    return jnp.concatenate([eye_block, eye_block], axis=0) / math.sqrt(2.0)


def column_products(left, right):
    return lax.dot_general(
        left,
        right,
        (((0,), (0,)), ((), ())),
        precision=lax.Precision.HIGHEST,
        preferred_element_type=jnp.float32,
    )


def same_gram(gram, level_bit):
    return gram


def replicated_basis(joined, combine_group, level_bit):
    local_gram = lax.dot_general(
        joined, joined, (((0,), (0,)), ((), ())), preferred_element_type=jnp.float32
    )
    gram = lax.psum(local_gram, "space")
    gram = combine_group(gram, level_bit)
    rotation = start_basis(joined.shape[1] // 2)
    for sweep_idx in range(ITERS):
        projected = jnp.dot(gram, rotation, precision=lax.Precision.HIGHEST)
        scaled = projected / jnp.sqrt(jnp.sum(projected * projected) + 1e-06)
        for inner_idx in range(NS_STEPS):
            moment = column_products(scaled, scaled)
            scaled = 1.5 * scaled - 0.5 * jnp.dot(scaled, moment, precision=lax.Precision.HIGHEST)
        rotation = scaled
    return rotation


def find_basis(joined, combine_group, level_bit):
    return replicated_basis(joined, combine_group, level_bit)


def body(snapshots, run_counts, route_counts):
    width = snapshots.shape[1]
    keep_cols = jnp.arange(width, dtype=jnp.int32) < run_counts[0]
    snap_data = jnp.where(keep_cols[None, :], snapshots, jnp.zeros((), snapshots.dtype))
    factor = route_rows(snap_data, route_counts)
    groups = lax.axis_size("run")
    levels = groups.bit_length() - 1
    run_index = lax.axis_index("run")
    quarter = width // groups
    for level_bit in range(levels):
        partner_block = swapped(factor, "run", level_bit)
        is_first = run_index >> level_bit & 1 == 0
        joined = jnp.where(
            is_first,
            jnp.concatenate([factor, partner_block], axis=1),
            jnp.concatenate([partner_block, factor], axis=1),
        )
        rotation = find_basis(joined, same_gram, level_bit)
        factor = jnp.dot(
            joined, rotation.astype(jnp.bfloat16), preferred_element_type=jnp.float32
        ).astype(jnp.bfloat16)
    result = lax.dynamic_slice_in_dim(factor, run_index * quarter, quarter, 1)
    return result


def solution(mesh):
    in_specs = (P("space", "run"), P("run"), P())
    out_specs = P("space", "run")
    return jax.shard_map(body, mesh=mesh, in_specs=in_specs, out_specs=out_specs, check_vma=False)
```

profile of v0, /device:TPU:1, one launch (start us, length us, event | category | flops | bytes accessed | tf_op | source)
XLA Modules:
  0.0 577.3 jit_solution(12328512857357104458)
XLA Ops:
  9.2 1.3 broadcast_select_fusion
  10.5 11.1 %gather_fusion = bf16[3072,256]{1,0:T(8,128)(2,1)S(1)} fusion(bf16[2048,256]{1,0:T(8,128)(2,1)S(1)} %broadcast_select_fusion, s32[3072]{0:T(1024)S(1)} %broadcast_clamp_fusion), kind=kCustom, calls=%fused_computation | custom fusion | bytes 3158016 | tf_op jit(solution)/shard_map/jit(_take)/gather | solution.py:32
  21.6 2.4 select_select_fusion
  23.9 13.1 %all-to-all-start = ((bf16[64,48,256]{2,1,0:T(8,128)(2,1)}), bf16[64,48,256]{2,1,0:T(8,128)(2,1)S(1)}, u32[]{:S(2)}, u32[]{:S(2)}) async-start(bf16[64,48,256]{2,1,0:T(8,128)(2,1)} %select_select_fusion), calls=%async_computation | async-start | bytes 3145728 | tf_op jit(solution)/shard_map/all_to_all | solution.py:35
  37.8 38.3 %all-to-all-done = bf16[64,48,256]{2,1,0:T(8,128)(2,1)S(1)} async-done(((bf16[64,48,256]{2,1,0:T(8,128)(2,1)}), bf16[64,48,256]{2,1,0:T(8,128)(2,1)S(1)}, u32[]{:S(2)}, u32[]{:S(2)}) %all-to-all-start) | async-done | bytes 1572896 | tf_op jit(solution)/shard_map/all_to_all | solution.py:35
  76.1 7.5 %gather_fusion.1 = bf16[2048,256]{1,0:T(8,128)(2,1)S(1)} fusion(bf16[3072,256]{1,0:T(8,128)(2,1)S(1)} %bitcast.137, s32[2048]{0:T(1024)S(1)} %broadcast_clamp_fusion.1), kind=kCustom, calls=%fused_computation.1 | custom fusion | bytes 2105344 | tf_op jit(solution)/shard_map/gather | solution.py:43
  83.6 1.4 collective-permute-start
  85.0 21.8 %collective-permute-done = bf16[2048,256]{1,0:T(8,128)(2,1)S(1)} collective-permute-done((bf16[2048,256]{1,0:T(8,128)(2,1)S(1)}, bf16[2048,256]{1,0:T(8,128)(2,1)S(1)}, u32[]{:S(2)}, u32[]{:S(2)}) %collective-permute-start) | collective-permute-done | bytes 1048608 | tf_op jit(solution)/shard_map/ppermute | solution.py:19
  106.7 2.3 fusion.38
  109.3 182.4 %all-reduce.3.cloned.1.call-done = f32[512,512]{1,0:T(8,128)} async-done(((f32[512,512]{1,0:T(8,128)}), f32[512,512]{1,0:T(8,128)}) %all-reduce.3.cloned.1.call-update) | async-done | bytes 1048592 | tf_op jit(solution)/shard_map/psum | solution.py:69
  291.8 2.8 multiply_reduce_fusion.3
  296.9 1.0 fusion.63
  298.6 1.0 fusion.64
  300.2 1.0 fusion.65
  301.9 1.0 fusion.66
  303.5 1.0 fusion.67
  305.1 1.0 fusion.68
  306.2 1.0 fusion.25
  307.2 1.0 fusion.69
  308.9 1.6 multiply_reduce_fusion.2
  312.8 1.0 fusion.70
  314.4 1.0 fusion.71
  316.1 1.0 fusion.72
  317.7 1.0 fusion.73
  319.4 1.0 fusion.74
  321.2 1.0 fusion.75
  322.8 1.0 fusion.76
  325.3 2.8 collective-permute-start.1
  328.1 21.2 %collective-permute-done.1 = bf16[2048,256]{0,1:T(8,128)(2,1)S(1)} collective-permute-done((bf16[2048,256]{0,1:T(8,128)(2,1)S(1)}, bf16[2048,256]{0,1:T(8,128)(2,1)S(1)}, u32[]{:S(2)}, u32[]{:S(2)}) %collective-permute-start.1) | collective-permute-done | bytes 1048608 | tf_op jit(solution)/shard_map/ppermute | solution.py:19
  349.3 2.3 fusion.40
  351.6 184.4 %all-reduce.5.cloned.1.call-done = f32[512,512]{1,0:T(8,128)} async-done(((f32[512,512]{1,0:T(8,128)}), f32[512,512]{1,0:T(8,128)}) %all-reduce.5.cloned.1.call-update) | async-done | bytes 1048592 | tf_op jit(solution)/shard_map/psum | solution.py:69
  536.0 2.8 multiply_reduce_fusion.1
  539.6 1.0 fusion.47
  541.2 1.0 fusion.77
  542.8 1.0 fusion.78
  544.5 1.0 fusion.79
  546.1 1.0 fusion.80
  547.7 1.0 fusion.81
  549.4 1.2 fusion.82
  551.2 1.0 fusion.83
  552.9 1.6 multiply_reduce_fusion
  556.8 1.0 fusion.84
  558.4 1.0 fusion.85
  560.1 1.0 fusion.86
  561.7 1.0 fusion.87
  563.3 1.3 fusion.88
  565.2 1.0 fusion.89
  566.9 1.0 fusion.90
  (74 shorter events, 26.6 us)
Async XLA Ops:
  23.9 13.2 %copy-start.2 = (s32[64,64]{1,0:T(8,128)S(1)}, s32[64,64]{1,0:T(8,128)}, u32[]{:S(2)}) copy-start(s32[64,64]{1,0:T(8,128)} %param.5) | copy-start | bytes 49156
  23.9 52.1 %all-to-all-start = ((bf16[64,48,256]{2,1,0:T(8,128)(2,1)}), bf16[64,48,256]{2,1,0:T(8,128)(2,1)S(1)}, u32[]{:S(2)}, u32[]{:S(2)}) async-start(bf16[64,48,256]{2,1,0:T(8,128)(2,1)} %select_select_fusion), calls=%async_computation | async-start | bytes 3145728 | tf_op jit(solution)/shard_map/all_to_all | solution.py:35
  37.1 254.7 %all-reduce.3.cloned.1.call-start = ((), (), s32[]{:S(2)}) async-start(), calls=%async_computation.1 | async-start | bytes 2097152 | tf_op jit(solution)/shard_map/psum | solution.py:69
  83.6 23.2 %collective-permute-start = (bf16[2048,256]{1,0:T(8,128)(2,1)S(1)}, bf16[2048,256]{1,0:T(8,128)(2,1)S(1)}, u32[]{:S(2)}, u32[]{:S(2)}) collective-permute-start(bf16[2048,256]{1,0:T(8,128)(2,1)S(1)} %gather_fusion.1), channel_id=1, source_target_pairs={{0,64},{64,0},{128,192},{192,128},{1,65},{65,1},{129,193},{193,129... | collective-permute-start | bytes 3145736 | tf_op jit(solution)/shard_map/ppermute | solution.py:19
  106.7 2.3 copy-start.5
  109.0 427.0 %all-reduce.5.cloned.1.call-start = ((), (), s32[]{:S(2)}) async-start(), calls=%async_computation.2 | async-start | bytes 2097152 | tf_op jit(solution)/shard_map/psum | solution.py:69
  307.2 1.7 copy-start.1
  322.2 2.2 copy-start.6
  325.3 26.3 %copy-start.3 = (bf16[2048,256]{0,1:T(8,128)(2,1)}, bf16[2048,256]{0,1:T(8,128)(2,1)S(1)}, u32[]{:S(2)}) copy-start(bf16[2048,256]{0,1:T(8,128)(2,1)S(1)} %convolution_convert_fusion) | copy-start | bytes 3145732
  325.3 24.0 %collective-permute-start.1 = (bf16[2048,256]{0,1:T(8,128)(2,1)S(1)}, bf16[2048,256]{0,1:T(8,128)(2,1)S(1)}, u32[]{:S(2)}, u32[]{:S(2)}) collective-permute-start(bf16[2048,256]{0,1:T(8,128)(2,1)S(1)} %convolution_convert_fusion), channel_id=1, source_target_pairs={{0,128},{128,0},{64,192},{192,64},{1,129},{129,1},{65,193},{193,65... | collective-permute-start | bytes 3145736 | tf_op jit(solution)/shard_map/ppermute | solution.py:19
  551.2 1.7 copy-start
  566.3 2.2 copy-start.4
Sparse Core Ops, SparseCore 0:
  109.2 182.5 all-reduce.2
  351.7 184.2 all-reduce.4
where the time goes:
time: 582 us; the launch traced here: 577 us
  waiting for transfers between devices  448 us (77%)
  matrix products  68 us (12%)
  local copies, waits for them, and re-layouts  20.3 us (3%)
  between operations  18 us (3%)
  starting transfers between devices  17.6 us (3%)
    psum x2, waiting for transfers between devices, replicated_basis(): gram = lax.psum(local_gram, 'space')  367 us
    ppermute x2, waiting for transfers between devices, swapped(): return lax.ppermute(block, axis, route)  42.9 us
    all_to_all x1, waiting for transfers between devices, route_rows(): lax.all_to_all(outgoing, 'space', split_axis=0, concat_axis=0, tiled=True)  38.3 us
    dot_general x32, matrix products, column_products(): lax.dot_general(left, right, (((0,), (0,)), ((), ())), precision=lax.Prec...  33.7 us
    dot_general x32, matrix products, replicated_basis(): jnp.dot(scaled, moment, precision=lax.Precision.HIGHEST)  19.3 us
    all_to_all x1, starting transfers between devices, route_rows(): lax.all_to_all(outgoing, 'space', split_axis=0, concat_axis=0, tiled=True)  13.1 us
  transfers between devices with their start and end apart: 5, of which 5 were waited for; matrix products, arithmetic and copies ran while one was open for 0% of the time, Pallas kernels for 0%

commit v1 on v0

v1 whole, which is shorter than its diff:
```python
import functools
import math

import jax
import jax.numpy as jnp
from jax import lax
from jax.experimental import pallas as pl
from jax.experimental.pallas import tpu as pltpu
from jax.sharding import PartitionSpec as P

ITERS = 2
NS_STEPS = 8
BF = jnp.bfloat16
F32 = jnp.float32


def dot(a, b):
    return lax.dot_general(a, b, (((1,), (0,)), ((), ())), preferred_element_type=F32)


def dot_t(a, b):
    return lax.dot_general(a, b, (((0,), (0,)), ((), ())), preferred_element_type=F32)


def split(x):
    hi = x.astype(BF)
    return hi, (x - hi.astype(F32)).astype(BF)


def mul(a, b, op=dot):
    return op(a[0], b[0]) + (op(a[0], b[1]) + op(a[1], b[0]))


def half_mul(a, b, op=dot):
    return op(a[0], b) + op(a[1], b)


def half_mul_t(b, a):
    return dot_t(b, a[0]) + dot_t(b, a[1])


def solve(grams, eye, m_ref, t_ref):
    count = len(grams)
    root = 1.0 / math.sqrt(2.0)
    gs = [(split(a), split(b), split(c)) for a, b, c in grams]
    heads = [((a + b) * root, (b.T + c) * root) for a, b, c in grams]
    for sweep in range(ITERS):
        if sweep:
            nxt = []
            for (a, b, c), (xt, xb) in zip(gs, heads):
                st, sb = split(xt), split(xb)
                nxt.append((mul(a, st) + mul(b, sb), mul(b, st, dot_t) + mul(c, sb)))
            heads = nxt
        scaled = []
        for i, (pt, pb) in enumerate(heads):
            norm = jnp.sqrt(jnp.sum(pt * pt + pb * pb, keepdims=True) + 1e-06)
            st, sb = split(pt / norm), split(pb / norm)
            scaled.append((st, sb))
            moment = mul(st, st, dot_t) + mul(sb, sb, dot_t)
            m_ref[i] = moment
            t_ref[i] = eye

        def step(_, carry):
            for i in range(count):
                moment = m_ref[i]
                sm = split(moment)
                weight = 1.5 * eye - 0.5 * moment
                square = mul(sm, sm)
                t_ref[i] = mul(split(t_ref[i]), split(weight))
                m_ref[i] = mul(sm, split(2.25 * eye - 1.5 * moment + 0.25 * square))
            return carry

        lax.fori_loop(0, NS_STEPS - 1, step, 0)
        heads = []
        for i in range(count):
            weight = 1.5 * eye - 0.5 * m_ref[i]
            turn = split(mul(split(t_ref[i]), split(weight)))
            st, sb = scaled[i]
            heads.append((mul(st, turn), mul(sb, turn)))
    return heads


def eig_kernel(place_ref, *refs):
    parts, (own_ref, far_ref, last_ref, gram_ref, m_ref, t_ref, sems) = refs[:8], refs[8:]
    run, core = place_ref[0], place_ref[1]
    copies = []
    for j in range(4):
        for k in range(2):
            slot = core if k == 0 else 1 - core
            copies.append(pltpu.make_async_copy(parts[2 * j + k], gram_ref.at[j, slot], sems.at[2 * j + k]))
    for c in copies:
        c.start()
    for c in copies:
        c.wait()
    width = own_ref.shape[1]
    half = width // 2
    rows = lax.broadcasted_iota(jnp.int32, (width, width), 0)
    cols = lax.broadcasted_iota(jnp.int32, (width, width), 1)
    eye = (rows == cols).astype(F32)

    def diag(j):
        return gram_ref[j, 0, :, :width]

    def edge(j):
        return jnp.concatenate([gram_ref[j, 0, :, width:], gram_ref[j, 1, :, :half]], axis=1)

    def cross(j):
        return gram_ref[j, 1, :, half:]

    near = (diag(0), edge(0), diag(1))
    far = (diag(2), edge(2), diag(3))
    bases = [(t.astype(BF), b.astype(BF)) for t, b in solve([near, far], eye, m_ref, t_ref)]
    for ref, (t, b) in zip((own_ref, far_ref), bases):
        ref[:width] = t
        ref[width:] = b

    def turned(gram, basis):
        a, b, c = (split(g) for g in gram)
        t, s = basis
        up = half_mul(a, t) + half_mul(b, s)
        down = half_mul(b, t, dot_t) + half_mul(c, s)
        return half_mul_t(t, split(up)) + half_mul_t(s, split(down))

    def between(first, second, f0, f1, s0, s1):
        (ft, fb), (st, sb) = first, second
        to_s1, to_s0 = split(cross(f0)), split(cross(f1))
        from_s0, from_s1 = split(cross(s0)), split(cross(s1))
        up = half_mul(to_s1, sb) + half_mul(from_s1, st, dot_t)
        down = half_mul(to_s0, st) + half_mul(from_s0, sb, dot_t)
        return half_mul_t(ft, split(up)) + half_mul_t(fb, split(down))

    a1 = turned(near, bases[0])
    c1 = turned(far, bases[1])

    @pl.when(run < 2)
    def _():
        m_ref[0] = between(bases[0], bases[1], 0, 1, 2, 3)

    @pl.when(run >= 2)
    def _():
        m_ref[0] = between(bases[1], bases[0], 2, 3, 0, 1).T

    b1 = m_ref[0]
    [(t, b)] = solve([(a1, b1, c1)], eye, m_ref, t_ref)
    lanes = last_ref.shape[1]
    quarter = lanes // 2
    pick_row = lax.broadcasted_iota(jnp.int32, (width, lanes), 0)
    pick_col = lax.broadcasted_iota(jnp.int32, (width, lanes), 1)
    pick_col = jnp.where(pick_col >= quarter, pick_col - quarter, pick_col)
    pick = (pick_row == pick_col + run * quarter).astype(F32).astype(BF)
    last_ref[:width] = dot(t.astype(BF), pick).astype(BF)
    last_ref[width:] = dot(b.astype(BF), pick).astype(BF)


def eig(place, parts, width):
    return pl.pallas_call(
        eig_kernel,
        out_shape=[
            jax.ShapeDtypeStruct((2 * width, width), BF),
            jax.ShapeDtypeStruct((2 * width, width), BF),
            jax.ShapeDtypeStruct((2 * width, width // 2), BF),
        ],
        in_specs=[pl.BlockSpec(memory_space=pltpu.SMEM)] + [pl.BlockSpec(memory_space=pl.ANY)] * 8,
        scratch_shapes=[
            pltpu.VMEM((4, 2, width, 3 * width // 2), F32),
            pltpu.VMEM((2, width, width), F32),
            pltpu.VMEM((2, width, width), F32),
            pltpu.SemaphoreType.DMA((8,)),
        ],
        compiler_params=pltpu.CompilerParams(vmem_limit_bytes=40 * 2**20),
        cost_estimate=pl.CostEstimate(flops=20 * 10**9, bytes_accessed=4 * 2**20, transcendentals=0),
        name="eigensolves",
    )(place, *parts)


def pack_kernel(shards, slots, counts_ref, own_ref, p1_ref, p2a_ref, p2b_ref, p3_ref, near_ref, far_ref, last_ref,
                out_ref, rows_ref, slot_ref):
    width = own_ref.shape[1]
    cells = own_ref.shape[0]
    tile = 512
    for k in range(cells // tile):
        at = pl.ds(k * tile, tile)
        half = cells // 2
        p2 = p2a_ref[at] if k * tile < half else p2b_ref[pl.ds(k * tile - half, tile)]
        near = (dot(own_ref[at], near_ref[:width]) + dot(p1_ref[at], near_ref[width:])).astype(BF)
        far = (dot(p2, far_ref[:width]) + dot(p3_ref[at], far_ref[width:])).astype(BF)
        rows_ref[at] = dot(near, last_ref[:width]) + dot(far, last_ref[width:])
    pad = rows_ref.shape[0] - cells
    rows_ref[pl.ds(cells, pad)] = jnp.zeros((pad, rows_ref.shape[1]), F32)
    half_slot = slots // 2
    lane = lax.broadcasted_iota(jnp.int32, (half_slot, rows_ref.shape[1]), 1)

    def one(d, start):
        first = rows_ref[pl.ds(start, half_slot)]
        second = rows_ref[pl.ds(start + half_slot, half_slot)]
        slot_ref[pl.ds(pl.multiple_of(d * half_slot, 8), half_slot)] = jnp.where(
            lane < rows_ref.shape[1] // 2, first, second
        )
        return jnp.minimum(start + counts_ref[d], cells)

    lax.fori_loop(0, shards, one, jnp.int32(0))
    out_ref[...] = slot_ref[...].astype(BF)


def unpack_kernel(shards, slots, counts_ref, in_ref, out_ref, slot_ref, rows_ref):
    cells, quarter = out_ref.shape
    half_slot = slots // 2
    slot_ref[...] = in_ref[...].astype(F32)

    def one(s, start):
        pair = slot_ref[pl.ds(pl.multiple_of(s * half_slot, 8), half_slot)]
        rows_ref[pl.ds(start, half_slot)] = pair
        rows_ref[pl.ds(start + half_slot, half_slot)] = pltpu.roll(pair, quarter, 1)
        return jnp.minimum(start + counts_ref[s], cells)

    lax.fori_loop(0, shards, one, jnp.int32(0))
    out_ref[...] = rows_ref[pl.ds(0, cells), :quarter].astype(BF)


def body(snapshots, run_counts, route_counts):
    cells, width = snapshots.shape
    shards = lax.axis_size("space")
    runs = lax.axis_size("run")
    slots = 3 * cells // (2 * shards)
    run = lax.axis_index("run")
    spot = lax.axis_index("space")
    core = lax.rem(spot, 2)
    groups = [[2 * i + c for i in range(shards // 2)] for c in range(2)]

    def across(x, mask):
        return lax.ppermute(x, "run", [(r, r ^ mask) for r in range(runs)])

    def other_core(x):
        return lax.ppermute(x, "space", [(s, s ^ 1) for s in range(shards)])

    def opposite(p1, p3):
        half = p1.shape[0] // 2
        return across(p1[:half], 3), across(p3[half:], 1)

    keep = jnp.arange(width, dtype=jnp.int32) < run_counts[0]
    own = jnp.where(keep[None, :], snapshots, jnp.zeros((), BF))
    p1, p3 = across(own, 1), across(own, 3)
    p2a, p2b = opposite(p1, p3)

    left = jnp.where(run < 2, own, p1)
    local = jnp.concatenate([dot_t(own, own), dot_t(own, p1), dot_t(left, p3)], axis=1)
    cut = local.shape[1] // 2
    mine = jnp.where(core == 0, local[:, :cut], local[:, cut:])
    theirs = jnp.where(core == 0, local[:, cut:], local[:, :cut])
    mine = mine + other_core(theirs)
    pieces = mine.reshape(shards // 2, -1, cut)
    pieces = lax.all_to_all(pieces, "space", 0, 0, tiled=True, axis_index_groups=groups)
    total = jnp.sum(pieces, axis=0)
    pieces = lax.all_to_all(
        jnp.broadcast_to(total, pieces.shape), "space", 0, 0, tiled=True, axis_index_groups=groups
    )
    g0 = pieces.reshape(width, cut)
    g1, g3 = across(g0, 1), across(g0, 3)
    g2 = jnp.concatenate(opposite(g1, g3), axis=0)
    parts = []
    for g in (g0, g1, g2, g3):
        parts += [g, other_core(g)]
    place = jnp.stack([run, core]).astype(jnp.int32)
    near, far, last = eig(place, parts, width)

    send = lax.dynamic_index_in_dim(route_counts, spot, 0, keepdims=False)
    recv = lax.dynamic_index_in_dim(route_counts, spot, 1, keepdims=False)
    smem = pl.BlockSpec(memory_space=pltpu.SMEM)
    vmem = pl.BlockSpec(memory_space=pltpu.VMEM)
    lanes = width // 2
    flat = shards * slots // 2
    packed = pl.pallas_call(
        functools.partial(pack_kernel, shards, slots),
        out_shape=jax.ShapeDtypeStruct((flat, lanes), BF),
        in_specs=[smem] + [vmem] * 8,
        out_specs=vmem,
        scratch_shapes=[pltpu.VMEM((cells + 64, lanes), F32), pltpu.VMEM((flat, lanes), F32)],
        compiler_params=pltpu.CompilerParams(vmem_limit_bytes=40 * 2**20),
        name="rotate_and_pack",
    )(send, own, p1, p2a, p2b, p3, near, far, last)
    arrived = lax.all_to_all(packed.reshape(shards, slots // 2, lanes), "space", 0, 0, tiled=True)
    return pl.pallas_call(
        functools.partial(unpack_kernel, shards, slots),
        out_shape=jax.ShapeDtypeStruct((cells, width // runs), BF),
        in_specs=[smem, vmem],
        out_specs=vmem,
        scratch_shapes=[pltpu.VMEM((flat, lanes), F32), pltpu.VMEM((cells + 64, lanes), F32)],
        compiler_params=pltpu.CompilerParams(vmem_limit_bytes=40 * 2**20),
        name="unpack",
    )(recv, arrived.reshape(flat, lanes))


def solution(mesh):
    in_specs = (P("space", "run"), P("run"), P())
    out_specs = P("space", "run")
    return jax.shard_map(body, mesh=mesh, in_specs=in_specs, out_specs=out_specs, check_vma=False)
```

time: 582 us -> 171 us (0.29)
  waiting for transfers between devices: 448 us -> 43.9 us
  matrix products: 68 us -> 1.57 us
  Pallas kernels: 0 us -> 43.5 us
  blocking collectives: 0 us -> 42.8 us
  between operations: 18 us -> 0.82 us
  local copies, waits for them, and re-layouts: 20.3 us -> 7.14 us
  starting transfers between devices: 17.6 us -> 27.5 us
    psum x2 -> x0, waiting for transfers between devices: 367 us -> none  [replicated_basis(): gram = lax.psum(local_gram, 'space')]
    dot_general x72 -> x3, matrix products: 68 us -> 1.57 us  [dot_t(): lax.dot_general(a, b, (((0,), (0,)), ((), ())), preferred_element_type=F32)]
    pallas_call x0 -> x3, Pallas kernels: none -> 43.5 us  [the longest x1 35 us: eig(): pl.pallas_call(eig_kernel, out_shape=[jax.ShapeDtypeStruct((2 * width, wi...]
    all_to_all x0 -> x2, blocking collectives: none -> 42.8 us  [the longest x1 25 us: body(): lax.all_to_all(pieces, 'space', 0, 0, tiled=True, axis_index_groups=groups)]
    all_to_all x1, waiting for transfers between devices: 38.3 us -> 14.9 us  [body(): lax.all_to_all(packed.reshape(shards, slots // 2, lanes), 'space', 0, 0,...]
    gather x2 -> x0, local copies, waits for them, and re-layouts: 18.5 us -> none  [the longest x1 11.1 us: route_rows(): jnp.take(rows_in, jnp.clip(pick_rows, 0, cell_count - 1).reshape(-1), axi...]
    ppermute x2 -> x13, starting transfers between devices: 4.19 us -> 21 us  [the longest x5 11.8 us: other_core(): return lax.ppermute(x, 'space', [(s, s ^ 1) for s in range(shards)])]
    ppermute x2 -> x13, waiting for transfers between devices: 42.9 us -> 29 us  [the longest x8 27.3 us: across(): return lax.ppermute(x, 'run', [(r, r ^ mask) for r in range(runs)])]
  transfers between devices with their start and end apart: 5 -> 14, of which waited for: 5 -> 6; matrix products, arithmetic and copies ran while one was open for 0% -> 3% of each run, Pallas kernels for 0% -> 21%
where the time goes in v1:
time: 171 us; the launch traced here: 170 us
  waiting for transfers between devices  43.9 us (26%)
  Pallas kernels  43.5 us (25%)
  blocking collectives  42.8 us (25%)
  starting transfers between devices  27.5 us (16%)
  local copies, waits for them, and re-layouts  7.14 us (4%)
  other arithmetic  3.29 us (2%)
    pallas_call x1, Pallas kernels, eig(): pl.pallas_call(eig_kernel, out_shape=[jax.ShapeDtypeStruct((2 * width, wi...  35 us
    ppermute x8, waiting for transfers between devices, across(): return lax.ppermute(x, 'run', [(r, r ^ mask) for r in range(runs)])  27.3 us
    all_to_all x1, blocking collectives, body(): lax.all_to_all(pieces, 'space', 0, 0, tiled=True, axis_index_groups=groups)  25 us
    all_to_all x1, blocking collectives, body(): lax.all_to_all(jnp.broadcast_to(total, pieces.shape), 'space', 0, 0, tile...  17.7 us
    all_to_all x1, waiting for transfers between devices, body(): lax.all_to_all(packed.reshape(shards, slots // 2, lanes), 'space', 0, 0,...  14.9 us
    ppermute x5, starting transfers between devices, other_core(): return lax.ppermute(x, 'space', [(s, s ^ 1) for s in range(shards)])  11.8 us
    ppermute x8, starting transfers between devices, across(): return lax.ppermute(x, 'run', [(r, r ^ mask) for r in range(runs)])  9.26 us
    all_to_all x1, starting transfers between devices, body(): lax.all_to_all(packed.reshape(shards, slots // 2, lanes), 'space', 0, 0,...  6.49 us
  transfers between devices with their start and end apart: 14, of which 6 were waited for; matrix products, arithmetic and copies ran while one was open for 3% of the time, Pallas kernels for 21%

profile of v1, /device:TPU:1, one launch (start us, length us, event | category | flops | bytes accessed | tf_op | source)
XLA Modules:
  0.0 170.4 jit_solution(17795596829849333352)
XLA Ops:
  0.7 1.3 broadcast_select_fusion.own_ref
  2.0 2.2 %collective-permute-start = (bf16[2048,256]{1,0:T(8,128)(2,1)S(1)}, bf16[2048,256]{1,0:T(8,128)(2,1)S(1)}, u32[]{:S(2)}, u32[]{:S(2)}) collective-permute-start(bf16[2048,256]{1,0:T(8,128)(2,1)S(1)} %broadcast_select_fusion.own_ref), channel_id=1, source_target_pairs={{0,64},{64,0},{128,192},{192,128},{1,65},{65,1},{129,193},{193,129... | collective-permute-start | bytes 3145736 | tf_op jit(solution)/shard_map/ppermute | solution.py:231
  4.2 1.9 %collective-permute-start.2 = (bf16[2048,256]{1,0:T(8,128)(2,1)S(1)}, bf16[2048,256]{1,0:T(8,128)(2,1)S(1)}, u32[]{:S(2)}, u32[]{:S(2)}) collective-permute-start(bf16[2048,256]{1,0:T(8,128)(2,1)S(1)} %broadcast_select_fusion.own_ref), channel_id=1, source_target_pairs={{0,192},{64,128},{128,64},{192,0},{1,193},{65,129},{129,65},{193,1... | collective-permute-start | bytes 3145736 | tf_op jit(solution)/shard_map/ppermute | solution.py:231
  6.1 0.5 fusion.4
  6.6 19.2 %collective-permute-done.p1_ref = bf16[2048,256]{1,0:T(8,128)(2,1)S(1)} collective-permute-done((bf16[2048,256]{1,0:T(8,128)(2,1)S(1)}, bf16[2048,256]{1,0:T(8,128)(2,1)S(1)}, u32[]{:S(2)}, u32[]{:S(2)}) %collective-permute-start) | collective-permute-done | bytes 1048608 | tf_op jit(solution)/shard_map/ppermute | solution.py:231
  25.8 0.5 fusion.5
  26.4 2.5 %collective-permute-done.2.p3_ref = bf16[2048,256]{1,0:T(8,128)(2,1)S(1)} collective-permute-done((bf16[2048,256]{1,0:T(8,128)(2,1)S(1)}, bf16[2048,256]{1,0:T(8,128)(2,1)S(1)}, u32[]{:S(2)}, u32[]{:S(2)}) %collective-permute-start.2) | collective-permute-done | bytes 1048608 | tf_op jit(solution)/shard_map/ppermute | solution.py:231
  28.8 0.5 fusion
  29.4 0.1 fusion.3
  29.4 2.2 %collective-permute-start.4 = (f32[256,384]{0,1:T(8,128)S(1)}, f32[256,384]{0,1:T(8,128)S(1)}, u32[]{:S(2)}, u32[]{:S(2)}) collective-permute-start(f32[256,384]{0,1:T(8,128)S(1)} %fusion.3), channel_id=1, source_target_pairs={{0,1},{1,0},{2,3},{3,2},{4,5},{5,4},{6,7},{7,6},{8,9},{9,8},{10,11... | collective-permute-start | bytes 1179656 | tf_op jit(solution)/shard_map/ppermute | solution.py:234
  31.7 1.3 collective-permute-done.4
  33.0 0.8 select_add_fusion
  33.8 1.9 %copy.5 = f32[256,384]{1,0:T(8,128)} copy(f32[256,384]{0,1:T(8,128)} %select_add_fusion) | data formatting | bytes 786432 | tf_op jit(solution)/shard_map/add | solution.py:250
  35.7 25.0 %all_to_all.15 = f32[32,8,384]{2,1,0:T(8,128)} all-to-all(f32[32,8,384]{2,1,0:T(8,128)} %bitcast.17), channel_id=1, replica_groups={{0,2,4,6,8,10,12,14,16,18,20,22,24,26,28,30,32,34,36,38,40,42,44,46,48,..., dimensions={0} | all-to-all | bytes 786432 | tf_op jit(solution)/shard_map/all_to_all | solution.py:252
  60.7 1.0 reduce_sum.9
  61.8 17.7 %all_to_all.16 = f32[32,8,384]{2,1,0:T(8,128)} all-to-all(f32[32,8,384]{2,1,0:T(8,128)S(1)} %broadcast_in_dim.18), channel_id=1, replica_groups={{0,2,4,6,8,10,12,14,16,18,20,22,24,26,28,30,32,34,36,38,40,42,44,46,48,..., dimensions={0} | all-to-all | bytes 786432 | tf_op jit(solution)/shard_map/all_to_all | solution.py:254
  79.6 0.0 collective-permute-start.6
  79.6 1.9 %collective-permute-start.9 = (f32[256,384]{1,0:T(8,128)}, f32[256,384]{1,0:T(8,128)}, u32[]{:S(2)}, u32[]{:S(2)}) collective-permute-start(f32[256,384]{1,0:T(8,128)} %bitcast.5.refs_0_), channel_id=1, source_target_pairs={{0,192},{64,128},{128,64},{192,0},{1,193},{65,129},{129,65},{193,1... | collective-permute-start | bytes 1179656 | tf_op jit(solution)/shard_map/ppermute | solution.py:231
  81.5 5.6 %collective-permute-done.6.refs_2_ = f32[256,384]{1,0:T(8,128)} collective-permute-done((f32[256,384]{1,0:T(8,128)}, f32[256,384]{1,0:T(8,128)}, u32[]{:S(2)}, u32[]{:S(2)}) %collective-permute-start.6) | collective-permute-done | bytes 393248 | tf_op jit(solution)/shard_map/ppermute | solution.py:231
  87.1 0.9 slice.30
  88.0 2.0 %collective-permute-start.8 = (f32[128,384]{1,0:T(8,128)S(1)}, f32[128,384]{1,0:T(8,128)S(1)}, u32[]{:S(2)}, u32[]{:S(2)}) collective-permute-start(f32[128,384]{1,0:T(8,128)S(1)} %slice.30), channel_id=1, source_target_pairs={{0,192},{64,128},{128,64},{192,0},{1,193},{65,129},{129,65},{193,1... | collective-permute-start | bytes 589832 | tf_op jit(solution)/shard_map/ppermute | solution.py:231
  90.0 0.0 collective-permute-done.9.refs_6_
  90.0 0.9 slice.31
  91.0 0.1 collective-permute-start.10
  91.1 4.7 %collective-permute-start.5 = (f32[256,384]{1,0:T(8,128)}, f32[256,384]{1,0:T(8,128)}, u32[]{:S(2)}, u32[]{:S(2)}) collective-permute-start(f32[256,384]{1,0:T(8,128)} %bitcast.5.refs_0_), channel_id=1, source_target_pairs={{0,1},{1,0},{2,3},{3,2},{4,5},{5,4},{6,7},{7,6},{8,9},{9,8},{10,11... | collective-permute-start | bytes 1179656 | tf_op jit(solution)/shard_map/ppermute | solution.py:234
  95.8 0.1 collective-permute-start.12
  95.9 0.4 collective-permute-start.7
  96.3 0.0 collective-permute-done.8
  96.3 0.7 constant_dynamic-update-slice_fusion.1
  97.0 0.0 collective-permute-done.10
  97.0 0.7 constant_dynamic-update-slice_fusion.refs_4_
  97.7 4.3 %collective-permute-start.11 = (f32[256,384]{1,0:T(8,128)}, f32[256,384]{1,0:T(8,128)}, u32[]{:S(2)}, u32[]{:S(2)}) collective-permute-start(f32[256,384]{1,0:T(8,128)} %constant_dynamic-update-slice_fusion.refs_4_), channel_id=1, source_target_pairs={{0,1},{1,0},{2,3},{3,2},{4,5},{5,4},{6,7},{7,6},{8,9},{9,8},{10,11... | collective-permute-start | bytes 1179656 | tf_op jit(solution)/shard_map/ppermute | solution.py:234
  102.0 0.1 pad_add_fusion.place_ref
  102.2 0.9 collective-permute-start.1
  103.1 0.0 collective-permute-done.5.refs_1_
  103.1 0.3 collective-permute-start.3
  103.4 0.0 collective-permute-done.12.refs_7_
  103.4 0.0 collective-permute-done.7.refs_3_
  103.4 0.3 collective-permute-done.11.refs_5_
  103.7 35.0 %eigensolves.1 = (bf16[512,256]{1,0:T(8,128)(2,1)S(1)}, bf16[512,256]{1,0:T(8,128)(2,1)S(1)}, bf16[512,128]{1,0:T(8,128)(2,1)S(1)}) custom-call(s32[2]{0:T(128)S(1)} %pad_add_fusion.place_ref, f32[256,384]{1,0:T(8,128)} %bitcast.5.refs_0_, f32[256,384]{1,0:T(8,128)} %collective-permute-done.5.refs_1_, f32[256,384]{1,0:T(8,128)} %collective-permute-done.6.refs_2_, ...), custom_call_target="tpu_custom_call" | custom-call | flops 20000000000 | bytes 4194304 | tf_op jit(solution)/shard_map/eigensolves/pallas_call | solution.py:156
  138.7 0.0 collective-permute-done.1.p2a_ref
  138.7 3.3 %rotate_and_pack.1 = bf16[1536,128]{1,0:T(8,128)(2,1)S(1)} custom-call(s32[64]{0:T(128)S(1)} %dynamic-slice_bitcast_fusion.counts_ref, bf16[2048,256]{1,0:T(8,128)(2,1)S(1)} %broadcast_select_fusion.own_ref, bf16[2048,256]{1,0:T(8,128)(2,1)S(1)} %collective-permute-done.p1_ref, bf16[1024,256]{1,0:T(8,128)(2,1)S(1)} %collective-permute-done.1.p2a_ref, ...), custom_call_target="tpu_custom_call" | custom-call | tf_op jit(solution)/shard_map/rotate_and_pack/pallas_call | solution.py:272
  142.1 0.7 copy-done.1
  142.8 6.5 %all-to-all-start.2 = ((bf16[64,24,128]{2,1,0:T(8,128)(2,1)}), bf16[64,24,128]{2,1,0:T(8,128)(2,1)S(1)}, u32[]{:S(2)}, u32[]{:S(2)}) async-start(bf16[64,24,128]{2,1,0:T(8,128)(2,1)} %bitcast.16), calls=%async_computation.2 | async-start | bytes 786432 | tf_op jit(solution)/shard_map/all_to_all | solution.py:281
  149.3 0.2 dynamic-slice_reduce_fusion.counts_ref
  149.5 14.9 %all-to-all-done.2 = bf16[64,24,128]{2,1,0:T(8,128)(2,1)S(1)} async-done(((bf16[64,24,128]{2,1,0:T(8,128)(2,1)}), bf16[64,24,128]{2,1,0:T(8,128)(2,1)S(1)}, u32[]{:S(2)}, u32[]{:S(2)}) %all-to-all-start.2) | async-done | bytes 393248 | tf_op jit(solution)/shard_map/all_to_all | solution.py:281
  164.3 5.2 %unpack.1 = bf16[2048,64]{1,0:T(8,128)(2,1)S(1)} custom-call(s32[64]{0:T(128)S(1)} %dynamic-slice_reduce_fusion.counts_ref, bf16[1536,128]{1,0:T(8,128)(2,1)S(1)} %bitcast.15), custom_call_target="tpu_custom_call" | custom-call | tf_op jit(solution)/shard_map/unpack/pallas_call | solution.py:282
  169.5 0.9 copy.6
  (9 shorter events, 0.1 us)
Async XLA Ops:
  0.0 102.1 %copy-start = (s32[64,64]{1,0:T(8,128)S(1)}, s32[64,64]{1,0:T(8,128)}, u32[]{:S(2)}) copy-start(s32[64,64]{1,0:T(8,128)} %param.5) | copy-start | bytes 49156
  2.0 23.8 %collective-permute-start = (bf16[2048,256]{1,0:T(8,128)(2,1)S(1)}, bf16[2048,256]{1,0:T(8,128)(2,1)S(1)}, u32[]{:S(2)}, u32[]{:S(2)}) collective-permute-start(bf16[2048,256]{1,0:T(8,128)(2,1)S(1)} %broadcast_select_fusion.own_ref), channel_id=1, source_target_pairs={{0,64},{64,0},{128,192},{192,128},{1,65},{65,1},{129,193},{193,129... | collective-permute-start | bytes 3145736 | tf_op jit(solution)/shard_map/ppermute | solution.py:231
  4.2 24.6 %collective-permute-start.2 = (bf16[2048,256]{1,0:T(8,128)(2,1)S(1)}, bf16[2048,256]{1,0:T(8,128)(2,1)S(1)}, u32[]{:S(2)}, u32[]{:S(2)}) collective-permute-start(bf16[2048,256]{1,0:T(8,128)(2,1)S(1)} %broadcast_select_fusion.own_ref), channel_id=1, source_target_pairs={{0,192},{64,128},{128,64},{192,0},{1,193},{65,129},{129,65},{193,1... | collective-permute-start | bytes 3145736 | tf_op jit(solution)/shard_map/ppermute | solution.py:231
  29.4 3.6 %collective-permute-start.4 = (f32[256,384]{0,1:T(8,128)S(1)}, f32[256,384]{0,1:T(8,128)S(1)}, u32[]{:S(2)}, u32[]{:S(2)}) collective-permute-start(f32[256,384]{0,1:T(8,128)S(1)} %fusion.3), channel_id=1, source_target_pairs={{0,1},{1,0},{2,3},{3,2},{4,5},{5,4},{6,7},{7,6},{8,9},{9,8},{10,11... | collective-permute-start | bytes 1179656 | tf_op jit(solution)/shard_map/ppermute | solution.py:234
  79.6 7.5 %collective-permute-start.6 = (f32[256,384]{1,0:T(8,128)}, f32[256,384]{1,0:T(8,128)}, u32[]{:S(2)}, u32[]{:S(2)}) collective-permute-start(f32[256,384]{1,0:T(8,128)} %bitcast.5.refs_0_), channel_id=1, source_target_pairs={{0,64},{64,0},{128,192},{192,128},{1,65},{65,1},{129,193},{193,129... | collective-permute-start | bytes 1179656 | tf_op jit(solution)/shard_map/ppermute | solution.py:231
  79.6 10.5 %collective-permute-start.9 = (f32[256,384]{1,0:T(8,128)}, f32[256,384]{1,0:T(8,128)}, u32[]{:S(2)}, u32[]{:S(2)}) collective-permute-start(f32[256,384]{1,0:T(8,128)} %bitcast.5.refs_0_), channel_id=1, source_target_pairs={{0,192},{64,128},{128,64},{192,0},{1,193},{65,129},{129,65},{193,1... | collective-permute-start | bytes 1179656 | tf_op jit(solution)/shard_map/ppermute | solution.py:231
  88.0 8.2 %collective-permute-start.8 = (f32[128,384]{1,0:T(8,128)S(1)}, f32[128,384]{1,0:T(8,128)S(1)}, u32[]{:S(2)}, u32[]{:S(2)}) collective-permute-start(f32[128,384]{1,0:T(8,128)S(1)} %slice.30), channel_id=1, source_target_pairs={{0,192},{64,128},{128,64},{192,0},{1,193},{65,129},{129,65},{193,1... | collective-permute-start | bytes 589832 | tf_op jit(solution)/shard_map/ppermute | solution.py:231
  91.0 6.0 %collective-permute-start.10 = (f32[128,384]{1,0:T(8,128)S(1)}, f32[128,384]{1,0:T(8,128)S(1)}, u32[]{:S(2)}, u32[]{:S(2)}) collective-permute-start(f32[128,384]{1,0:T(8,128)S(1)} %slice.31), channel_id=1, source_target_pairs={{0,64},{64,0},{128,192},{192,128},{1,65},{65,1},{129,193},{193,129... | collective-permute-start | bytes 589832 | tf_op jit(solution)/shard_map/ppermute | solution.py:231
  91.1 12.0 %collective-permute-start.5 = (f32[256,384]{1,0:T(8,128)}, f32[256,384]{1,0:T(8,128)}, u32[]{:S(2)}, u32[]{:S(2)}) collective-permute-start(f32[256,384]{1,0:T(8,128)} %bitcast.5.refs_0_), channel_id=1, source_target_pairs={{0,1},{1,0},{2,3},{3,2},{4,5},{5,4},{6,7},{7,6},{8,9},{9,8},{10,11... | collective-permute-start | bytes 1179656 | tf_op jit(solution)/shard_map/ppermute | solution.py:234
  95.8 7.6 %collective-permute-start.12 = (f32[256,384]{1,0:T(8,128)}, f32[256,384]{1,0:T(8,128)}, u32[]{:S(2)}, u32[]{:S(2)}) collective-permute-start(f32[256,384]{1,0:T(8,128)} %collective-permute-done.9.refs_6_), channel_id=1, source_target_pairs={{0,1},{1,0},{2,3},{3,2},{4,5},{5,4},{6,7},{7,6},{8,9},{9,8},{10,11... | collective-permute-start | bytes 1179656 | tf_op jit(solution)/shard_map/ppermute | solution.py:234
  95.9 7.5 %collective-permute-start.7 = (f32[256,384]{1,0:T(8,128)}, f32[256,384]{1,0:T(8,128)}, u32[]{:S(2)}, u32[]{:S(2)}) collective-permute-start(f32[256,384]{1,0:T(8,128)} %collective-permute-done.6.refs_2_), channel_id=1, source_target_pairs={{0,1},{1,0},{2,3},{3,2},{4,5},{5,4},{6,7},{7,6},{8,9},{9,8},{10,11... | collective-permute-start | bytes 1179656 | tf_op jit(solution)/shard_map/ppermute | solution.py:234
  97.7 6.0 %collective-permute-start.11 = (f32[256,384]{1,0:T(8,128)}, f32[256,384]{1,0:T(8,128)}, u32[]{:S(2)}, u32[]{:S(2)}) collective-permute-start(f32[256,384]{1,0:T(8,128)} %constant_dynamic-update-slice_fusion.refs_4_), channel_id=1, source_target_pairs={{0,1},{1,0},{2,3},{3,2},{4,5},{5,4},{6,7},{7,6},{8,9},{9,8},{10,11... | collective-permute-start | bytes 1179656 | tf_op jit(solution)/shard_map/ppermute | solution.py:234
  102.2 36.6 %collective-permute-start.1 = (bf16[1024,256]{1,0:T(8,128)(2,1)S(1)}, bf16[1024,256]{1,0:T(8,128)(2,1)S(1)}, u32[]{:S(2)}, u32[]{:S(2)}) collective-permute-start(bf16[1024,256]{1,0:T(8,128)(2,1)S(1)} %slice.28), channel_id=1, source_target_pairs={{0,192},{64,128},{128,64},{192,0},{1,193},{65,129},{129,65},{193,1... | collective-permute-start | bytes 1572872 | tf_op jit(solution)/shard_map/ppermute | solution.py:231
  103.1 35.7 %collective-permute-start.3 = (bf16[1024,256]{1,0:T(8,128)(2,1)S(1)}, bf16[1024,256]{1,0:T(8,128)(2,1)S(1)}, u32[]{:S(2)}, u32[]{:S(2)}) collective-permute-start(bf16[1024,256]{1,0:T(8,128)(2,1)S(1)} %slice.29), channel_id=1, source_target_pairs={{0,64},{64,0},{128,192},{192,128},{1,65},{65,1},{129,193},{193,129... | collective-permute-start | bytes 1572872 | tf_op jit(solution)/shard_map/ppermute | solution.py:231
  142.0 0.7 copy-start.1
  142.8 21.6 %all-to-all-start.2 = ((bf16[64,24,128]{2,1,0:T(8,128)(2,1)}), bf16[64,24,128]{2,1,0:T(8,128)(2,1)S(1)}, u32[]{:S(2)}, u32[]{:S(2)}) async-start(bf16[64,24,128]{2,1,0:T(8,128)(2,1)} %bitcast.16), calls=%async_computation.2 | async-start | bytes 786432 | tf_op jit(solution)/shard_map/all_to_all | solution.py:281
